TPU v7x, 512 devices: a whole 4x4x16 slice. The times are simulated.
512 devices in a mesh: node: 16 (over x, y_hi, core), dp: 32 (over z, y_lo).
Axes of the slice: x: 4, y: 4 (y_hi: 2, y_lo: 2; y = y_hi * 2 + y_lo), z: 16, core: 2. Of those that a mesh axis runs over, the one named last changes fastest.
Arguments:
- tokens_in: bfloat16 [65536, 8192], P(('node', 'dp')), may hold values from -4 to 4
- gain: float32 [8192], replicated, may hold values from 0.5 to 1.5
- value_weight: bfloat16 [8192, 512], P('node'), may hold values from -1 to 1
- value_grad: bfloat16 [65536, 512], P(('node', 'dp')), may hold values from -0.24 to 0.24
Outputs:
- weight_grad: float32 [8192, 512], P(('node', 'dp'))
- gain_grad: float32 [8192], P(('node', 'dp'))
- input_grad: bfloat16 [65536, 8192], P(('node', 'dp'))
All inputs are finite; a program needn't handle non-finite values.
Results may differ from a plain program's by a relative error of at most 0.035.
Values may be sent and summed in bfloat16 or wider, within the bound.
A program may use at most 64 MiB of HBM per device.

v0:
```python
import jax
import jax.numpy as jnp
from jax import lax
from jax.sharding import PartitionSpec as P

D = 8192


EPS = 1e-05


def normalize(tokens_in, gain):
    tokens_f32 = tokens_in.astype(jnp.float32)
    inv_rms = lax.rsqrt(jnp.mean(tokens_f32 * tokens_f32, axis=1, keepdims=True) + EPS)
    unit = tokens_f32 * inv_rms
    normed = unit.astype(jnp.bfloat16)
    scaled = (normed.astype(jnp.float32) * gain).astype(jnp.bfloat16)
    return (inv_rms, unit, normed, scaled)


def input_gradient(normed_grad, gain, inv_rms, unit):
    feature_grad = normed_grad * gain
    spread = jnp.mean(feature_grad * unit, axis=1, keepdims=True)
    return (inv_rms * (feature_grad - unit * spread)).astype(jnp.bfloat16)


def on_device(tokens_in, gain, value_weight, value_grad):
    out_cols = value_weight.shape[1]
    peer_count = lax.axis_size("node")
    block_rows = D // peer_count
    inv_rms, unit, normed, scaled = normalize(tokens_in, gain)
    normed_grad = lax.dot_general(
        value_grad,
        lax.all_gather(value_weight, "node", axis=0, tiled=True),
        (((1,), (1,)), ((), ())),
        preferred_element_type=jnp.float32,
    )
    gain_term = jnp.sum(normed.astype(jnp.float32) * normed_grad, axis=0).astype(jnp.bfloat16)

    def column_block(block_index):
        columns = lax.dynamic_slice_in_dim(scaled, block_index * block_rows, block_rows, 1)
        return lax.dot_general(
            columns, value_grad, (((0,), (0,)), ((), ())), preferred_element_type=jnp.float32
        ).astype(jnp.bfloat16)

    weight_term = lax.map(column_block, jnp.arange(peer_count, dtype=jnp.int32)).reshape(
        peer_count * block_rows, out_cols
    )
    weight_mix, gain_mix = (
        lax.all_to_all(weight_term, "node", split_axis=0, concat_axis=0, tiled=True),
        lax.all_to_all(gain_term, "node", split_axis=0, concat_axis=0, tiled=True),
    )
    weight_sum = (
        weight_mix.astype(jnp.float32).reshape(peer_count, block_rows, out_cols).sum(axis=0)
    )
    gain_sum = gain_mix.astype(jnp.float32).reshape(peer_count, block_rows).sum(axis=0)
    input_grad = input_gradient(normed_grad, gain, inv_rms, unit)
    weight_group = lax.optimization_barrier(weight_sum.astype(jnp.bfloat16))
    gain_group = lax.optimization_barrier(gain_sum.astype(jnp.bfloat16))
    weight_mix, gain_mix = (
        lax.all_to_all(weight_group, "dp", split_axis=0, concat_axis=0, tiled=True),
        lax.all_to_all(gain_group, "dp", split_axis=0, concat_axis=0, tiled=True),
    )
    group_count = lax.axis_size("dp")
    sub_rows = block_rows // group_count
    weight_grad = (
        weight_mix.astype(jnp.float32).reshape(group_count, sub_rows, out_cols).sum(axis=0)
    )
    gain_grad = gain_mix.astype(jnp.float32).reshape(group_count, sub_rows).sum(axis=0)
    return (weight_grad, gain_grad, input_grad)


def solution(mesh):
    placed = (P(("node", "dp"), None), P(), P("node", None), P(("node", "dp"), None))
    return jax.shard_map(
        on_device,
        mesh=mesh,
        in_specs=placed,
        out_specs=(P(("node", "dp"), None), P(("node", "dp")), P(("node", "dp"), None)),
        check_vma=False,
    )
```

profile of v0, /device:TPU:28, one launch (start us, length us, event | category | flops | bytes accessed | tf_op | source)
XLA Modules:
  0.0 390.5 jit_solution(16810289533650198830)
XLA Ops:
  7.2 0.0 all-gather.2.cloned.1.call-start
  7.2 0.7 all-gather.2.cloned.1.call-update
  7.9 2.1 fusion.11
  10.0 0.0 copy-start
  10.0 0.0 copy-start.2
  10.0 90.4 %all-gather.2.cloned.1.call-done = bf16[8192,512]{1,0:T(8,128)(2,1)} async-done(((bf16[512,512]{1,0:T(8,128)(2,1)}), bf16[8192,512]{1,0:T(8,128)(2,1)}) %all-gather.2.cloned.1.call-update) | async-done | bytes 8388624 | tf_op jit(solution)/shard_map/all_gather | solution.py:34
  100.4 8.8 %fusion.7 = (f32[128]{0:T(128)S(1)}, bf16[8192]{0:T(1024)(128)(2,1)S(1)}, f32[128,8192]{1,0:T(8,128)}) fusion(bf16[128,8192]{1,0:T(8,128)(2,1)} %param.6, f32[8192]{0:T(1024)} %param.7, f32[128]{0:T(128)S(1)} %add_rsqrt_fusion, bf16[128,512]{1,0:T(8,128)(2,1)} %param.9, bf16[8192,512]{1,0:T(8,128)(2,1)} %all-gather.2.cloned.1.call-done), kind=kOutput, calls=%fused_computation.12 | convolution fusion | flops 1083170688 | bytes 14861312 | tf_op jit(solution)/shard_map/dot_general | solution.py:32
  109.3 0.5 broadcast.24
  109.8 0.7 reduce.4
  110.6 0.6 reshape.49
  111.2 7.2 %all-to-all-start.2 = ((bf16[16,2,256]{2,1,0:T(2,128)(2,1)}), bf16[16,2,256]{2,1,0:T(2,128)(2,1)S(1)}, u32[]{:S(2)}, u32[]{:S(2)}) async-start(bf16[16,2,256]{2,1,0:T(2,128)(2,1)} %reshape.49), calls=%async_computation.2 | async-start | bytes 32768 | tf_op jit(solution)/shard_map/all_to_all | solution.py:51
  118.4 0.0 copy-done
  118.4 0.0 copy-done.2
  118.4 0.0 copy-start.1
  118.4 5.5 %fusion.10 = (bf16[128,8192]{1,0:T(8,128)(2,1)}, bf16[128,8192]{1,0:T(8,128)(2,1)}) fusion(bf16[128,8192]{1,0:T(8,128)(2,1)S(1)} %copy-done, f32[128,8192]{1,0:T(8,128)} %get-tuple-element.45, f32[128]{0:T(128)S(1)} %broadcast_multiply_fusion, f32[8192]{0:T(1024)S(1)} %copy-done.2, f32[128]{0:T(128)S(1)} %add_rsqrt_fusion), kind=kLoop, calls=%fused_computation.15 | loop fusion | flops 11534336 | bytes 10519552 | tf_op jit(solution)/shard_map/convert_element_type | solution.py:24
  124.0 0.0 copy-done.1
  124.0 53.7 %while.10 = (s32[]{:T(128)}, bf16[16,512,512]{2,1,0:T(8,128)(2,1)}, s32[16]{0:T(128)S(1)}, bf16[128,8192]{1,0:T(8,128)(2,1)}, bf16[128,512]{1,0:T(8,128)(2,1)S(1...) while((s32[]{:T(128)}, bf16[16,512,512]{2,1,0:T(8,128)(2,1)}, s32[16]{0:T(128)S(1)}, ...), condition=%wide.region_2.3_spmd, body=%wide.region_1.0_spmd.sunk | while | flops 67371016 | bytes 786599 | solution.py:46
  124.0 0.6 dynamic_slice.12
  125.3 2.0 fusion.22
  127.3 0.6 dynamic_slice.12
  128.7 2.0 fusion.22
  130.7 0.6 dynamic_slice.12
  132.0 2.0 fusion.22
  134.1 0.6 dynamic_slice.12
  135.4 2.0 fusion.22
  137.4 0.6 dynamic_slice.12
  138.7 2.0 fusion.22
  140.8 0.6 dynamic_slice.12
  142.1 2.0 fusion.22
  144.1 0.6 dynamic_slice.12
  145.5 2.0 fusion.22
  147.5 0.6 dynamic_slice.12
  148.8 2.0 fusion.22
  150.8 0.6 dynamic_slice.12
  152.2 2.0 fusion.22
  154.2 0.6 dynamic_slice.12
  155.5 2.1 fusion.22
  157.6 0.6 dynamic_slice.12
  158.9 2.0 fusion.22
  160.9 0.6 dynamic_slice.12
  162.3 2.0 fusion.22
  164.3 0.6 dynamic_slice.12
  165.6 2.0 fusion.22
  167.7 0.6 dynamic_slice.12
  169.0 2.0 fusion.22
  171.0 0.6 dynamic_slice.12
  172.3 2.0 fusion.22
  174.4 0.6 dynamic_slice.12
  175.7 2.0 fusion.22
  177.7 0.0 all-to-all-done.2
  177.7 7.2 %all-to-all-start = ((bf16[16,512,512]{2,1,0:T(8,128)(2,1)}), bf16[16,512,512]{2,1,0:T(8,128)(2,1)}, u32[]{:S(2)}, u32[]{:S(2)}) async-start(bf16[16,512,512]{2,1,0:T(8,128)(2,1)} %get-tuple-element.30), calls=%async_computation | async-start | bytes 16777216 | tf_op jit(solution)/shard_map/all_to_all | solution.py:50
  185.0 0.1 bitcast_reduce_fusion
  185.0 0.7 all_to_all.26
  185.7 132.5 %all-to-all-done = bf16[16,512,512]{2,1,0:T(8,128)(2,1)} async-done(((bf16[16,512,512]{2,1,0:T(8,128)(2,1)}), bf16[16,512,512]{2,1,0:T(8,128)(2,1)}, u32[]{:S(2)}, u32[]{:S(2)}) %all-to-all-start) | async-done | bytes 8388640 | tf_op jit(solution)/shard_map/all_to_all | solution.py:50
  318.2 13.8 %all-to-all-start.3 = ((bf16[32,16,1]{1,2,0:T(2,128)(2,1)}), bf16[32,16,1]{1,2,0:T(2,128)(2,1)S(1)}, u32[]{:S(2)}, u32[]{:S(2)}) async-start(bf16[32,16,1]{1,2,0:T(2,128)(2,1)} %all_to_all.26), calls=%async_computation.3 | async-start | bytes 32768 | tf_op jit(solution)/shard_map/all_to_all | solution.py:62
  332.0 5.5 %reduce_sum.70 = bf16[512,512]{1,0:T(8,128)(2,1)} reduce(bf16[16,512,512]{2,1,0:T(8,128)(2,1)} %all-to-all-done, bf16[]{:T(256)} %constant.23.clone.1), dimensions={0}, to_apply=%region_3.4 | reduce | flops 3932160 | bytes 8912898 | tf_op jit(solution)/shard_map/reduce_sum | solution.py:54
  337.5 6.6 %all-to-all-done.3 = bf16[32,16,1]{1,2,0:T(2,128)(2,1)S(1)} async-done(((bf16[32,16,1]{1,2,0:T(2,128)(2,1)}), bf16[32,16,1]{1,2,0:T(2,128)(2,1)S(1)}, u32[]{:S(2)}, u32[]{:S(2)}) %all-to-all-start.3) | async-done | bytes 1056 | tf_op jit(solution)/shard_map/all_to_all | solution.py:62
  344.1 6.5 %all-to-all-start.1 = ((bf16[32,16,512]{2,1,0:T(8,128)(2,1)}), bf16[32,16,512]{2,1,0:T(8,128)(2,1)S(1)}, u32[]{:S(2)}, u32[]{:S(2)}) async-start(bf16[32,16,512]{2,1,0:T(8,128)(2,1)} %bitcast.2), calls=%async_computation.1 | async-start | bytes 1048576 | tf_op jit(solution)/shard_map/all_to_all | solution.py:61
  350.6 0.6 convert_reduce_fusion.1
  351.2 31.8 %all-to-all-done.1 = bf16[32,16,512]{2,1,0:T(8,128)(2,1)S(1)} async-done(((bf16[32,16,512]{2,1,0:T(8,128)(2,1)}), bf16[32,16,512]{2,1,0:T(8,128)(2,1)S(1)}, u32[]{:S(2)}, u32[]{:S(2)}) %all-to-all-start.1) | async-done | bytes 524320 | tf_op jit(solution)/shard_map/all_to_all | solution.py:61
  382.9 0.7 convert_reduce_fusion
  (6 shorter events, 0.0 us)
Async XLA Ops:
  7.2 93.3 %all-gather.2.cloned.1.call-start = ((), (), s32[]{:S(2)}) async-start(), calls=%async_computation.4 | async-start | bytes 8912896 | tf_op jit(solution)/shard_map/all_gather | solution.py:34
  10.0 108.4 %copy-start = (bf16[128,8192]{1,0:T(8,128)(2,1)S(1)}, bf16[128,8192]{1,0:T(8,128)(2,1)}, u32[]{:S(2)}) copy-start(bf16[128,8192]{1,0:T(8,128)(2,1)} %param.6) | copy-start | bytes 6291460
  10.0 108.4 %copy-start.2 = (f32[8192]{0:T(1024)S(1)}, f32[8192]{0:T(1024)}, u32[]{:S(2)}) copy-start(f32[8192]{0:T(1024)} %param.7) | copy-start | bytes 98308
  111.2 66.6 %all-to-all-start.2 = ((bf16[16,2,256]{2,1,0:T(2,128)(2,1)}), bf16[16,2,256]{2,1,0:T(2,128)(2,1)S(1)}, u32[]{:S(2)}, u32[]{:S(2)}) async-start(bf16[16,2,256]{2,1,0:T(2,128)(2,1)} %reshape.49), calls=%async_computation.2 | async-start | bytes 32768 | tf_op jit(solution)/shard_map/all_to_all | solution.py:51
  118.4 5.6 %copy-start.1 = (bf16[128,512]{1,0:T(8,128)(2,1)S(1)}, bf16[128,512]{1,0:T(8,128)(2,1)}, u32[]{:S(2)}) copy-start(bf16[128,512]{1,0:T(8,128)(2,1)} %param.9) | copy-start | bytes 393220
  177.7 140.5 %all-to-all-start = ((bf16[16,512,512]{2,1,0:T(8,128)(2,1)}), bf16[16,512,512]{2,1,0:T(8,128)(2,1)}, u32[]{:S(2)}, u32[]{:S(2)}) async-start(bf16[16,512,512]{2,1,0:T(8,128)(2,1)} %get-tuple-element.30), calls=%async_computation | async-start | bytes 16777216 | tf_op jit(solution)/shard_map/all_to_all | solution.py:50
  318.2 25.9 %all-to-all-start.3 = ((bf16[32,16,1]{1,2,0:T(2,128)(2,1)}), bf16[32,16,1]{1,2,0:T(2,128)(2,1)S(1)}, u32[]{:S(2)}, u32[]{:S(2)}) async-start(bf16[32,16,1]{1,2,0:T(2,128)(2,1)} %all_to_all.26), calls=%async_computation.3 | async-start | bytes 32768 | tf_op jit(solution)/shard_map/all_to_all | solution.py:62
  344.1 38.8 %all-to-all-start.1 = ((bf16[32,16,512]{2,1,0:T(8,128)(2,1)}), bf16[32,16,512]{2,1,0:T(8,128)(2,1)S(1)}, u32[]{:S(2)}, u32[]{:S(2)}) async-start(bf16[32,16,512]{2,1,0:T(8,128)(2,1)} %bitcast.2), calls=%async_computation.1 | async-start | bytes 1048576 | tf_op jit(solution)/shard_map/all_to_all | solution.py:61
Sparse Core Ops, SparseCore 0:
  11.3 89.1 all-gather.1
where the time goes:
time: 391 us; the launch traced here: 390 us
  waiting for transfers between devices  262 us (67%)
  matrix products  41.4 us (11%)
  starting transfers between devices  34.8 us (9%)
  other arithmetic  15.2 us (4%)
  between operations  14.1 us (4%)
  local copies, waits for them, and re-layouts  12.2 us (3%)
  loops' own time  10.9 us (3%)
    all_to_all x1, waiting for transfers between devices, on_device(): lax.all_to_all(weight_term, 'node', split_axis=0, concat_axis=0, tiled=True)  132 us
    all_gather x1, waiting for transfers between devices, on_device(): lax.all_gather(value_weight, 'node', axis=0, tiled=True)  90.4 us
    dot_general x16, matrix products, column_block(): lax.dot_general(columns, value_grad, (((0,), (0,)), ((), ())), preferred_...  32.6 us
    all_to_all x1, waiting for transfers between devices, on_device(): lax.all_to_all(weight_group, 'dp', split_axis=0, concat_axis=0, tiled=True)  31.8 us
    all_to_all x1, starting transfers between devices, on_device(): lax.all_to_all(gain_group, 'dp', split_axis=0, concat_axis=0, tiled=True)  13.8 us
    another operation x1, loops' own time, on_device(): lax.map(column_block, jnp.arange(peer_count, dtype=jnp.int32))  10.9 us
    dynamic_slice x16, local copies, waits for them, and re-layouts, on_device(): lax.map(column_block, jnp.arange(peer_count, dtype=jnp.int32))  10.3 us
    dot_general x1, matrix products, on_device(): lax.dot_general(value_grad, lax.all_gather(value_weight, 'node', axis=0,...  8.85 us
  transfers between devices with their start and end apart: 5, of which 4 were waited for; matrix products, arithmetic and copies ran while one was open for 14% of the time, Pallas kernels for 0%

commit v1 on v0

v1 whole, which is shorter than its diff:
```python
import jax
import jax.numpy as jnp
from jax import lax
from jax.experimental import pallas as pl
from jax.experimental.pallas import tpu as pltpu
from jax.sharding import PartitionSpec as P

D = 8192
EPS = 1e-05
NX, NY, NZ = 4, 4, 16
T = 128
K = 512
F = 256
BF, F32 = jnp.bfloat16, jnp.float32
MESH = pl.DeviceIdType.MESH


def device_at(x, y, z, core):
    return (x * 4 + (y // 2) * 2 + core, z * 2 + y % 2)


def kernel(
    tok_hbm, gain_ref, weight_hbm, vg_hbm,
    wg_ref, gg_ref, ig_hbm,
    tok, shard, vgall, inv, nsend, nall, wall, ngs, ngr,
    s1, s2, r1, r2, t1, t2, u1, u2, vb, zr, outb,
    load_sem, vg_s, vg_r, tok_s, tok_r, ax_s, ax_r, ay_s, ay_r, ap_s, ap_r,
    back_s, back_r, p1_s, p1_r, p2_s, p2_r, q1_s, q1_r, q2_s, q2_r, z_s, z_r, out_sem,
):
    node, dp = lax.axis_index("node"), lax.axis_index("dp")
    x, yh, c = node // 4, (node // 2) % 2, node % 2
    z, yl = dp // 2, dp % 2
    y = yh * 2 + yl
    p = z % 2
    zs = (z + 17 - 2 * c) % NZ
    zup, zdn = (z + 1) % NZ, (z + 15) % NZ
    me = lambda **kw: device_at(kw.get("x", x), kw.get("y", y), kw.get("z", z), kw.get("c", c))

    def send(src, dst, ssem, rsem, to):
        return pltpu.make_async_remote_copy(
            src_ref=src, dst_ref=dst, send_sem=ssem, recv_sem=rsem, device_id=to, device_id_type=MESH
        )

    load_tok = pltpu.make_async_copy(tok_hbm, tok, load_sem.at[0])
    load_w = pltpu.make_async_copy(weight_hbm, shard, load_sem.at[1])
    load_vg = pltpu.make_async_copy(vg_hbm, vgall.at[pl.ds(0, T)], load_sem.at[2])
    load_tok.start()
    load_w.start()
    load_vg.start()

    barrier = pltpu.get_barrier_semaphore()
    partners = [me(x=(x + d) % NX) for d in (1, 2, 3)] + [me(y=(y + d) % NY) for d in (1, 2, 3)]
    partners += [me(c=1 - c), me(z=zup, c=1 - c), me(z=zdn, c=1 - c)]
    for to in partners:
        pl.semaphore_signal(barrier, inc=1, device_id=to, device_id_type=MESH)

    def greet(d, carry):
        pl.semaphore_signal(barrier, inc=1, device_id=me(z=(z + d) % NZ), device_id_type=MESH)
        return carry

    lax.fori_loop(1, NZ, greet, 0)

    load_tok.wait()

    def squares(i, acc):
        t = tok[:, pl.ds(pl.multiple_of(i * K, K), K)].astype(F32)
        t = t * t
        return acc + ((t[:, 0:128] + t[:, 128:256]) + (t[:, 256:384] + t[:, 384:512]))

    acc = lax.fori_loop(0, D // K, squares, jnp.zeros((T, 128), F32))
    mean = jnp.sum(acc, axis=1, keepdims=True) * (1.0 / D)
    inv[...] = jnp.broadcast_to(lax.rsqrt(mean + EPS), (T, 128))

    def column(j, xt, ht):
        cc = c if j in (0, 2) else 1 - c
        pp = p if j < 2 else 1 - p
        return pl.multiple_of(xt * 2048 + ht * 1024 + cc * 512 + pp * 256, 256)

    def unit_tile(j, xt, ht):
        scale = inv[...]
        scale = jnp.concatenate([scale, scale], axis=1)
        return tok[:, pl.ds(column(j, xt, ht), F)].astype(F32) * scale

    load_w.wait()
    load_vg.wait()
    pl.semaphore_wait(barrier, len(partners) + NZ - 1)

    slot = 3 - c
    helpers = [(me(c=1 - c), 1), (me(z=zs), slot), (me(z=zs, c=1 - c), slot)]
    vg_copies = [
        send(vgall.at[pl.ds(0, T)], vgall.at[pl.ds(sl * T, T)], vg_s.at[i], vg_r.at[sl - 1], to)
        for i, (to, sl) in enumerate(helpers)
    ]
    for copy in vg_copies:
        copy.start()

    own_rows = pl.ds(pl.multiple_of(p * F, F), F)
    half = 1 - yl
    ax = [send(shard.at[own_rows], wall.at[x, yh], ax_s.at[d - 1], ax_r.at[d - 1], me(x=(x + d) % NX)) for d in (1, 2, 3)]
    out_half = pl.ds(pl.multiple_of(half * 128, 128), 128)
    in_half = pl.ds(pl.multiple_of(yl * 128, 128), 128)
    ay = [
        send(
            shard.at[pl.ds(pl.multiple_of(p * F + half * 128, 128), 128)] if d == 0 else wall.at[(x + d) % NX, yh, out_half],
            wall.at[(x + d) % NX, yh, out_half], ay_s.at[d], ay_r.at[d], me(y=3 - y),
        )
        for d in range(NX)
    ]
    ap = [
        send(
            wall.at[(x + d) % NX, 1 - yh, in_half], wall.at[(x + d) % NX, 1 - yh, in_half],
            ap_s.at[d], ap_r.at[d], me(y=yh * 2 + 1 - yl),
        )
        for d in range(NX)
    ]
    ay_in = [
        send(
            wall.at[(x + d) % NX, 1 - yh, in_half], wall.at[(x + d) % NX, 1 - yh, in_half],
            ay_s.at[d], ay_r.at[d], me(y=3 - y),
        )
        for d in range(NX)
    ]
    ay[0].start()
    ax[0].start()
    ax[2].start()
    ax[1].start()

    def token_copy(i, xt):
        to, sl = helpers[i]
        return send(
            nsend.at[i, xt], nall.at[xt, :, pl.ds(sl * T, T)], tok_s.at[i, xt], tok_r.at[sl - 1, xt], to
        )

    def normalize(m, carry):
        xt = (x + 2 + m) % NX
        for ht in range(2):
            for j in (2, 3, 1, 0):
                tile = unit_tile(j, xt, ht).astype(BF)
                if j == 0:
                    nall[xt, ht, 0:T] = tile
                else:
                    nsend[(0, 0, 1, 2)[j], xt, ht] = tile
        for i in (1, 2, 0):
            token_copy(i, xt).start()
        return carry

    lax.fori_loop(0, NX, normalize, 0)
    wall[x, yh] = shard[own_rows]

    for sl in (1, 2, 3):
        send(vgall.at[pl.ds(0, T)], vgall.at[pl.ds(sl * T, T)], vg_s.at[0], vg_r.at[sl - 1], me(c=1 - c)).wait_recv()

    def p1_copy(d, ht):
        return send(
            s1.at[(x + d) % NX, pl.ds(ht * 2, 2)], r1.at[d - 1, pl.ds(ht * 2, 2)],
            p1_s.at[d - 1, ht], p1_r.at[d - 1, ht], me(x=(x + d) % NX),
        )

    def p2_copy(e, xt):
        return send(
            s2.at[(y + e) % NY, xt], r2.at[e - 1, xt], p2_s.at[e - 1, xt], p2_r.at[e - 1, xt], me(y=(y + e) % NY)
        )

    def weight_tile(xt, ht):
        total = lax.dot_general(nall[xt, ht], vgall[...], (((0,), (0,)), ((), ())), preferred_element_type=F32)
        total = total.astype(BF).reshape(8, 2, 16, K)
        for low in range(2):
            part = total[:, low].reshape(128, K)
            s1[xt, ht * 2 + low] = part[:, 0:256]
            s2[ht * 2 + low, xt] = part[:, 256:512]

    def weight_step(m):
        d = (2 + m) % NX
        xt = (x + d) % NX
        for sl in (1, 2, 3):
            send(nsend.at[0, xt], nall.at[xt, :, pl.ds(sl * T, T)], tok_s.at[0, xt], tok_r.at[sl - 1, xt], me(c=1 - c)).wait_recv()

        def tiles(h, carry):
            ht = (yh + 1 + h) % 2
            weight_tile(xt, ht)
            if d != 0:
                p1_copy(d, ht).start()
            for low in range(2):
                e = (ht * 2 + low - y + NY) % NY

                @pl.when(e != 0)
                def _():
                    p2_copy(e, xt).start()

            return carry

        lax.fori_loop(0, 2, tiles, 0)

    for i in (0, 2):
        ax[i].wait_recv()
    ay[3].start()
    ay[1].start()
    weight_step(0)
    ay_in[0].wait_recv()
    ap[0].start()
    ax[1].wait_recv()
    ay[2].start()
    weight_step(1)
    for d in (1, 3):
        ay_in[d].wait_recv()
        ap[d].start()
    weight_step(2)
    weight_step(3)
    ay_in[2].wait_recv()
    ap[2].start()

    owners = [(me(c=1 - c), 1), (me(z=zup, c=1), 3 - c), (me(z=zdn, c=0), 2 + c)]

    def back_copy(i, xt):
        to, j = owners[i]
        return send(ngs.at[xt, :, pl.ds(i * T, T)], ngr.at[j, xt], back_s.at[i, xt], back_r.at[j - 1, xt], to)

    def grad_tiles(xt):
        def tiles(ht, carry):
            ng = lax.dot_general(
                vgall[...], wall[xt, ht], (((1,), (1,)), ((), ())), preferred_element_type=F32
            ).astype(BF)
            ngr[0, xt, ht] = ng[0:T]
            ngs[xt, ht] = ng[T:]
            return carry

        lax.fori_loop(0, 2, tiles, 0)
        for i in (1, 2, 0):
            back_copy(i, xt).start()

    for d in (0, 1, 3, 2):
        send(
            wall.at[(x + d) % NX, 1 - yh, out_half], wall.at[(x + d) % NX, 1 - yh, out_half],
            ap_s.at[d], ap_r.at[d], me(y=yh * 2 + 1 - yl),
        ).wait_recv()
        grad_tiles((x + d) % NX)

    def q1_copy(e):
        return send(t1.at[(y + e) % NY], u1.at[e - 1], q1_s.at[e - 1], q1_r.at[e - 1], me(y=(y + e) % NY))

    def q2_copy(d):
        return send(t2.at[(x + d) % NX], u2.at[d - 1], q2_s.at[d - 1], q2_r.at[d - 1], me(x=(x + d) % NX))

    for ht in range(2):
        for d in (1, 2, 3):
            p1_copy(d, ht).wait_recv()

    def add1(e, carry):
        yt = (y + e) % NY
        total = s1[x, yt].astype(F32) + r1[0, yt].astype(F32) + r1[1, yt].astype(F32) + r1[2, yt].astype(F32)
        t1[yt] = total.astype(BF)

        @pl.when(e != NY)
        def _():
            q1_copy(e).start()

        return carry

    lax.fori_loop(1, NY + 1, add1, 0)
    for xt in range(NX):
        for e in (1, 2, 3):
            p2_copy(e, xt).wait_recv()

    def add2(d, carry):
        xt = (x + d) % NX
        total = s2[y, xt].astype(F32) + r2[0, xt].astype(F32) + r2[1, xt].astype(F32) + r2[2, xt].astype(F32)
        t2[xt] = total.astype(BF)

        @pl.when(d != NX)
        def _():
            q2_copy(d).start()

        return carry

    lax.fori_loop(1, NX + 1, add2, 0)

    for e in (1, 2, 3):
        q1_copy(e).wait_recv()
    total = t1[y].astype(F32) + u1[0].astype(F32) + u1[1].astype(F32) + u1[2].astype(F32)
    vb[:, :, 0:256] = total.astype(BF).reshape(8, 16, 256)
    for d in (1, 2, 3):
        q2_copy(d).wait_recv()
    total = t2[x].astype(F32) + u2[0].astype(F32) + u2[1].astype(F32) + u2[2].astype(F32)
    vb[:, :, 256:512] = total.astype(BF).reshape(8, 16, 256)

    def z_copy(k):
        return send(vb.at[k], zr.at[z // 2], z_s.at[k], z_r.at[z // 2], me(z=p * 8 + k))

    def z_start(i, carry):
        k = (z + i) % 8

        @pl.when(p * 8 + k != z)
        def _():
            z_copy(k).start()

        @pl.when(p * 8 + k == z)
        def _():
            zr[z // 2] = vb[k]

        return carry

    lax.fori_loop(0, 8, z_start, 0)

    for j in (1, 2, 3):
        for xt in range(NX):
            send(ngs.at[xt, :, pl.ds(0, T)], ngr.at[j, xt], back_s.at[0, xt], back_r.at[j - 1, xt], me(c=1 - c)).wait_recv()

    def feature_tile(j, xt, ht):
        return ngr[j, xt, ht].astype(F32) * gain_ref[:, pl.ds(column(j, xt, ht), F)]

    def spread_tile(i, acc):
        xt, ht = i // 2, i % 2
        for j in range(4):
            prod = feature_tile(j, xt, ht) * unit_tile(j, xt, ht)
            acc = acc + (prod[:, 0:128] + prod[:, 128:256])
        return acc

    acc = lax.fori_loop(0, 8, spread_tile, jnp.zeros((T, 128), F32))
    spread = jnp.sum(acc, axis=1, keepdims=True) * (1.0 / D)

    def input_tile(i, carry):
        xt, ht = i // 2, i % 2
        scale = inv[...]
        scale = jnp.concatenate([scale, scale], axis=1)
        for j in range(4):
            grad = scale * (feature_tile(j, xt, ht) - unit_tile(j, xt, ht) * spread)
            outb[:, pl.ds(column(j, xt, ht), F)] = grad.astype(BF)
        return carry

    lax.fori_loop(0, 8, input_tile, 0)
    store = pltpu.make_async_copy(outb, ig_hbm, out_sem.at[0])
    store.start()

    def z_wait(k, carry):
        @pl.when(2 * k + z // 8 != z)
        def _():
            send(vb.at[k], zr.at[k], z_s.at[k], z_r.at[k], me(z=(z + 1) % NZ)).wait_recv()

        return carry

    lax.fori_loop(0, 8, z_wait, 0)
    total = zr[0].astype(F32)
    for k in range(1, 8):
        total = total + zr[k].astype(F32)

    lanes = lax.broadcasted_iota(jnp.int32, (16, 128), 1)
    rows = lax.broadcasted_iota(jnp.int32, (16, 128), 0)
    block = gain_ref[:, pl.ds(pl.multiple_of(node * 512 + (dp // 8) * 128, 128), 128)]
    picked = jnp.where(lanes == rows + (dp % 8) * 16, jnp.broadcast_to(block, (16, 128)), 0.0)
    wg_ref[...] = total * jnp.sum(picked, axis=1, keepdims=True)
    own = shard[pl.ds(pl.multiple_of(dp * 16, 16), 16)].astype(F32)
    gain_sum = jnp.sum(own * total, axis=1, keepdims=True)
    spread_out = jnp.where(lanes == rows, jnp.broadcast_to(gain_sum, (16, 128)), 0.0)
    gg_ref[...] = jnp.sum(spread_out, axis=0, keepdims=True)

    for copy in vg_copies + ax + ay + ap:
        copy.wait_send()
    for i in range(3):
        for xt in range(NX):
            token_copy(i, xt).wait_send()
            back_copy(i, xt).wait_send()
            p2_copy(i + 1, xt).wait_send()
        for ht in range(2):
            p1_copy(i + 1, ht).wait_send()
        q1_copy(i + 1).wait_send()
        q2_copy(i + 1).wait_send()

    def z_sent(k, carry):
        @pl.when(p * 8 + k != z)
        def _():
            z_copy(k).wait_send()

        return carry

    lax.fori_loop(0, 8, z_sent, 0)
    store.wait()


def on_device(tokens_in, gain, value_weight, value_grad):
    vmem, dma = pltpu.VMEM, pltpu.SemaphoreType.DMA
    scratch = [
        vmem((T, D), BF), vmem((K, K), BF), vmem((4 * T, K), BF), vmem((T, 128), F32),
        vmem((3, NX, 2, T, F), BF), vmem((NX, 2, 4 * T, F), BF), vmem((NX, 2, F, K), BF),
        vmem((NX, 2, 3 * T, F), BF), vmem((4, NX, 2, T, F), BF),
        vmem((NX, NY, 128, 256), BF), vmem((NY, NX, 128, 256), BF),
        vmem((3, NY, 128, 256), BF), vmem((3, NX, 128, 256), BF),
        vmem((NY, 128, 256), BF), vmem((NX, 128, 256), BF),
        vmem((3, 128, 256), BF), vmem((3, 128, 256), BF),
        vmem((8, 16, K), BF), vmem((8, 16, K), BF), vmem((T, D), BF),
    ]
    sems = [(3,)] + [(3,)] * 2 + [(3, NX)] * 2 + [(3,)] * 2 + [(4,)] * 4 + [(3, NX)] * 2
    sems += [(3, 2)] * 2 + [(3, NX)] * 2 + [(3,)] * 4 + [(8,)] * 2 + [(1,)]
    any_space = pl.BlockSpec(memory_space=pl.ANY)
    in_vmem = pl.BlockSpec(memory_space=pltpu.VMEM)
    weight_grad, gain_grad, input_grad = pl.pallas_call(
        kernel,
        out_shape=(
            jax.ShapeDtypeStruct((16, K), F32),
            jax.ShapeDtypeStruct((1, 128), F32),
            jax.ShapeDtypeStruct((T, D), BF),
        ),
        in_specs=[any_space, in_vmem, any_space, any_space],
        out_specs=(in_vmem, in_vmem, any_space),
        scratch_shapes=scratch + [dma(s) for s in sems],
        compiler_params=pltpu.CompilerParams(
            collective_id=0, has_side_effects=True, vmem_limit_bytes=48 * 1024 * 1024
        ),
    )(tokens_in, gain.reshape(1, D), value_weight, value_grad)
    return weight_grad, gain_grad[0, :16], input_grad


def solution(mesh):
    placed = (P(("node", "dp"), None), P(), P("node", None), P(("node", "dp"), None))
    return jax.shard_map(
        on_device,
        mesh=mesh,
        in_specs=placed,
        out_specs=(P(("node", "dp"), None), P(("node", "dp")), P(("node", "dp"), None)),
        check_vma=False,
    )
```

time: 391 us -> 72 us (0.18)
  the two profiles are of different devices: /device:TPU:28 before, /device:TPU:7 now
where the time goes in v1:
time: 72 us; the launch traced here: 71.8 us
  Pallas kernels  64.4 us (89%)
  local copies, waits for them, and re-layouts  6.73 us (9%)
    pallas_call x1, Pallas kernels, on_device(): pl.pallas_call(kernel, out_shape=(jax.ShapeDtypeStruct((16, K), F32), jax...  64.4 us
    unnamed x10, local copies, waits for them, and re-layouts  6.22 us

profile of v1, /device:TPU:7, one launch (start us, length us, event | category | flops | bytes accessed | tf_op | source)
XLA Modules:
  0.0 71.8 jit_solution(9358732941602601529)
XLA Ops:
  0.6 0.0 copy-start
  0.6 1.6 %copy-done = bf16[128,8192]{1,0:T(8,128)(2,1)S(1)} copy-done((bf16[128,8192]{1,0:T(8,128)(2,1)S(1)}, bf16[128,8192]{1,0:T(8,128)(2,1)}, u32[]{:S(2)}) %copy-start) | copy-done | bytes 2097176
  2.2 0.0 copy-start.1
  2.2 1.0 %copy-done.1 = bf16[512,512]{1,0:T(8,128)(2,1)S(1)} copy-done((bf16[512,512]{1,0:T(8,128)(2,1)S(1)}, bf16[512,512]{1,0:T(8,128)(2,1)}, u32[]{:S(2)}) %copy-start.1) | copy-done | bytes 524312
  3.3 0.0 copy-start.2
  3.3 0.9 %copy-done.2 = bf16[128,512]{1,0:T(8,128)(2,1)S(1)} copy-done((bf16[128,512]{1,0:T(8,128)(2,1)S(1)}, bf16[128,512]{1,0:T(8,128)(2,1)}, u32[]{:S(2)}) %copy-start.2) | copy-done | bytes 131096
  4.2 0.0 copy-start.3
  4.2 0.8 %copy-done.3 = f32[8192]{0:T(1024)S(1)} copy-done((f32[8192]{0:T(1024)S(1)}, f32[8192]{0:T(1024)}, u32[]{:S(2)}) %copy-start.3) | copy-done | bytes 32792
  4.9 64.4 %shard_map.67 = (f32[16,512]{1,0:T(8,128)S(1)}, f32[1,128]{1,0:T(1,128)S(1)}, bf16[128,8192]{1,0:T(8,128)(2,1)S(1)}) custom-call(bf16[128,8192]{1,0:T(8,128)(2,1)S(1)} %copy-done, f32[1,8192]{1,0:T(1,128)S(1)} %bitcast.3, bf16[512,512]{1,0:T(8,128)(2,1)S(1)} %copy-done.1, bf16[128,512]{1,0:T(8,128)(2,1)S(1)} %copy-done.2), custom_call_target="tpu_custom_call" | custom-call | tf_op jit(solution)/shard_map/pallas_call | solution.py:395
  69.3 0.5 slice_bitcast_fusion
  69.8 0.6 copy.9
  70.4 1.3 %copy.10 = bf16[128,8192]{1,0:T(8,128)(2,1)} copy(bf16[128,8192]{1,0:T(8,128)(2,1)S(1)} %get-tuple-element.14) | data formatting | bytes 4194304
Async XLA Ops:
  0.6 1.6 %copy-start = (bf16[128,8192]{1,0:T(8,128)(2,1)S(1)}, bf16[128,8192]{1,0:T(8,128)(2,1)}, u32[]{:S(2)}) copy-start(bf16[128,8192]{1,0:T(8,128)(2,1)} %tok_hbm.1) | copy-start | bytes 6291460
  2.2 1.0 %copy-start.1 = (bf16[512,512]{1,0:T(8,128)(2,1)S(1)}, bf16[512,512]{1,0:T(8,128)(2,1)}, u32[]{:S(2)}) copy-start(bf16[512,512]{1,0:T(8,128)(2,1)} %weight_hbm.1) | copy-start | bytes 1572868
  3.3 0.9 %copy-start.2 = (bf16[128,512]{1,0:T(8,128)(2,1)S(1)}, bf16[128,512]{1,0:T(8,128)(2,1)}, u32[]{:S(2)}) copy-start(bf16[128,512]{1,0:T(8,128)(2,1)} %vg_hbm.1) | copy-start | bytes 393220
  4.2 0.8 %copy-start.3 = (f32[8192]{0:T(1024)S(1)}, f32[8192]{0:T(1024)}, u32[]{:S(2)}) copy-start(f32[8192]{0:T(1024)} %param.5) | copy-start | bytes 98308

commit v2 on v1

--- a/solution.py
+++ b/solution.py
@@ -20,12 +20,12 @@
 
 
 def kernel(
-    tok_hbm, gain_ref, weight_hbm, vg_hbm,
-    wg_ref, gg_ref, ig_hbm,
-    tok, shard, vgall, inv, nsend, nall, wall, ngs, ngr,
-    s1, s2, r1, r2, t1, t2, u1, u2, vb, zr, outb,
+    tok_hbm, gain_hbm, weight_hbm, vg_hbm,
+    wg_ref, gg_ref, ig_ref,
+    tok, gain_ref, shard, vgall, inv, nsend, nall, wall, ngs, ngr,
+    s1, s2, r1, r2, t1, t2, u1, u2, vb, zr,
     load_sem, vg_s, vg_r, tok_s, tok_r, ax_s, ax_r, ay_s, ay_r, ap_s, ap_r,
-    back_s, back_r, p1_s, p1_r, p2_s, p2_r, q1_s, q1_r, q2_s, q2_r, z_s, z_r, out_sem,
+    back_s, back_r, p1_s, p1_r, p2_s, p2_r, q1_s, q1_r, q2_s, q2_r, z_s, z_r, near_sem, two_sem, four_sem,
 ):
     node, dp = lax.axis_index("node"), lax.axis_index("dp")
     x, yh, c = node // 4, (node // 2) % 2, node % 2
@@ -44,21 +44,21 @@
     load_tok = pltpu.make_async_copy(tok_hbm, tok, load_sem.at[0])
     load_w = pltpu.make_async_copy(weight_hbm, shard, load_sem.at[1])
     load_vg = pltpu.make_async_copy(vg_hbm, vgall.at[pl.ds(0, T)], load_sem.at[2])
+    load_gain = pltpu.make_async_copy(gain_hbm, gain_ref, load_sem.at[3])
     load_tok.start()
     load_w.start()
     load_vg.start()
+    load_gain.start()
 
     barrier = pltpu.get_barrier_semaphore()
     partners = [me(x=(x + d) % NX) for d in (1, 2, 3)] + [me(y=(y + d) % NY) for d in (1, 2, 3)]
-    partners += [me(c=1 - c), me(z=zup, c=1 - c), me(z=zdn, c=1 - c)]
+    partners += [me(c=1 - c), me(z=zup), me(z=zdn), me(z=zup, c=1 - c), me(z=zdn, c=1 - c)]
     for to in partners:
         pl.semaphore_signal(barrier, inc=1, device_id=to, device_id_type=MESH)
 
-    def greet(d, carry):
-        pl.semaphore_signal(barrier, inc=1, device_id=me(z=(z + d) % NZ), device_id_type=MESH)
-        return carry
-
-    lax.fori_loop(1, NZ, greet, 0)
+    def tell(sem, d):
+        for to in (me(z=(z + d) % NZ), me(z=(z + NZ - d) % NZ)):
+            pl.semaphore_signal(sem, inc=1, device_id=to, device_id_type=MESH)
 
     load_tok.wait()
 
@@ -83,16 +83,21 @@
 
     load_w.wait()
     load_vg.wait()
-    pl.semaphore_wait(barrier, len(partners) + NZ - 1)
+    load_gain.wait()
+    pl.semaphore_wait(barrier, len(partners))
+    tell(near_sem, 1)
 
     slot = 3 - c
     helpers = [(me(c=1 - c), 1), (me(z=zs), slot), (me(z=zs, c=1 - c), slot)]
-    vg_copies = [
-        send(vgall.at[pl.ds(0, T)], vgall.at[pl.ds(sl * T, T)], vg_s.at[i], vg_r.at[sl - 1], to)
-        for i, (to, sl) in enumerate(helpers)
-    ]
-    for copy in vg_copies:
-        copy.start()
+
+    def vg_copy(i, mine, to_slot, to):
+        return send(
+            vgall.at[pl.ds(mine * T, T)], vgall.at[pl.ds(to_slot * T, T)], vg_s.at[i], vg_r.at[to_slot - 1], to
+        )
+
+    vg_copies = [vg_copy(0, 0, 1, me(c=1 - c)), vg_copy(1, 0, slot, me(z=zs)), vg_copy(2, slot, slot, me(c=1 - c))]
+    vg_copies[0].start()
+    vg_copies[1].start()
 
     own_rows = pl.ds(pl.multiple_of(p * F, F), F)
     half = 1 - yl
@@ -140,15 +145,19 @@
                     nall[xt, ht, 0:T] = tile
                 else:
                     nsend[(0, 0, 1, 2)[j], xt, ht] = tile
-        for i in (1, 2, 0):
+        for i in (0, 1, 2):
             token_copy(i, xt).start()
         return carry
 
     lax.fori_loop(0, NX, normalize, 0)
     wall[x, yh] = shard[own_rows]
 
-    for sl in (1, 2, 3):
-        send(vgall.at[pl.ds(0, T)], vgall.at[pl.ds(sl * T, T)], vg_s.at[0], vg_r.at[sl - 1], me(c=1 - c)).wait_recv()
+    vg_copy(1, 0, slot, me(z=zs)).wait_recv()
+    vg_copies[2].start()
+    pl.semaphore_wait(near_sem, 2)
+    tell(two_sem, 2)
+    for sl in (1, 2 + c):
+        vg_copy(0, 0, sl, me(c=1 - c)).wait_recv()
 
     def p1_copy(d, ht):
         return send(
@@ -191,88 +200,99 @@
 
         lax.fori_loop(0, 2, tiles, 0)
 
+    owners = [(me(c=1 - c), 1), (me(z=zup, c=1), 3 - c), (me(z=zdn, c=0), 2 + c)]
+
+    def back_copy(i, xt, ht):
+        to, j = owners[i]
+        return send(
+            ngs.at[xt, ht, pl.ds(i * T, T)], ngr.at[j, xt, ht], back_s.at[i, xt, ht], back_r.at[j - 1, xt, ht], to
+        )
+
+    def grad_tile(xt, ht):
+        ng = lax.dot_general(
+            vgall[...], wall[xt, ht], (((1,), (1,)), ((), ())), preferred_element_type=F32
+        ).astype(BF)
+        ngr[0, xt, ht] = ng[0:T]
+        ngs[xt, ht] = ng[T:]
+        for i in range(3):
+            back_copy(i, xt, ht).start()
+
+    weight_step(0)
     for i in (0, 2):
         ax[i].wait_recv()
     ay[3].start()
     ay[1].start()
-    weight_step(0)
+    pl.semaphore_wait(two_sem, 2)
+    tell(four_sem, 4)
+    weight_step(1)
     ay_in[0].wait_recv()
     ap[0].start()
     ax[1].wait_recv()
     ay[2].start()
-    weight_step(1)
+    weight_step(2)
+    weight_step(3)
     for d in (1, 3):
         ay_in[d].wait_recv()
         ap[d].start()
-    weight_step(2)
-    weight_step(3)
+
+    def near_tile(i, carry):
+        grad_tile((x + i) % NX, yh)
+        return carry
+
+    lax.fori_loop(0, NX, near_tile, 0)
     ay_in[2].wait_recv()
     ap[2].start()
 
-    owners = [(me(c=1 - c), 1), (me(z=zup, c=1), 3 - c), (me(z=zdn, c=0), 2 + c)]
-
-    def back_copy(i, xt):
-        to, j = owners[i]
-        return send(ngs.at[xt, :, pl.ds(i * T, T)], ngr.at[j, xt], back_s.at[i, xt], back_r.at[j - 1, xt], to)
-
-    def grad_tiles(xt):
-        def tiles(ht, carry):
-            ng = lax.dot_general(
-                vgall[...], wall[xt, ht], (((1,), (1,)), ((), ())), preferred_element_type=F32
-            ).astype(BF)
-            ngr[0, xt, ht] = ng[0:T]
-            ngs[xt, ht] = ng[T:]
-            return carry
-
-        lax.fori_loop(0, 2, tiles, 0)
-        for i in (1, 2, 0):
-            back_copy(i, xt).start()
+    def q1_copy(e):
+        return send(t1.at[(y + e) % NY], u1.at[e - 1], q1_s.at[e - 1], q1_r.at[e - 1], me(y=(y + e) % NY))
+
+    def q2_copy(d):
+        return send(t2.at[(x + d) % NX], u2.at[d - 1], q2_s.at[d - 1], q2_r.at[d - 1], me(x=(x + d) % NX))
+
+    for ht in range(2):
+        for d in (1, 2, 3):
+            p1_copy(d, ht).wait_recv()
+
+    def add1(e, carry):
+        yt = (y + e) % NY
+        total = s1[x, yt].astype(F32) + r1[0, yt].astype(F32) + r1[1, yt].astype(F32) + r1[2, yt].astype(F32)
+        t1[yt] = total.astype(BF)
+
+        @pl.when(e != NY)
+        def _():
+            q1_copy(e).start()
+
+        return carry
+
+    lax.fori_loop(1, NY + 1, add1, 0)
+    for xt in range(NX):
+        for e in (1, 2, 3):
+            p2_copy(e, xt).wait_recv()
+
+    def add2(d, carry):
+        xt = (x + d) % NX
+        total = s2[y, xt].astype(F32) + r2[0, xt].astype(F32) + r2[1, xt].astype(F32) + r2[2, xt].astype(F32)
+        t2[xt] = total.astype(BF)
+
+        @pl.when(d != NX)
+        def _():
+            q2_copy(d).start()
+
+        return carry
+
+    lax.fori_loop(1, NX + 1, add2, 0)
 
     for d in (0, 1, 3, 2):
         send(
             wall.at[(x + d) % NX, 1 - yh, out_half], wall.at[(x + d) % NX, 1 - yh, out_half],
             ap_s.at[d], ap_r.at[d], me(y=yh * 2 + 1 - yl),
         ).wait_recv()
-        grad_tiles((x + d) % NX)
-
-    def q1_copy(e):
-        return send(t1.at[(y + e) % NY], u1.at[e - 1], q1_s.at[e - 1], q1_r.at[e - 1], me(y=(y + e) % NY))
-
-    def q2_copy(d):
-        return send(t2.at[(x + d) % NX], u2.at[d - 1], q2_s.at[d - 1], q2_r.at[d - 1], me(x=(x + d) % NX))
-
-    for ht in range(2):
-        for d in (1, 2, 3):
-            p1_copy(d, ht).wait_recv()
-
-    def add1(e, carry):
-        yt = (y + e) % NY
-        total = s1[x, yt].astype(F32) + r1[0, yt].astype(F32) + r1[1, yt].astype(F32) + r1[2, yt].astype(F32)
-        t1[yt] = total.astype(BF)
-
-        @pl.when(e != NY)
-        def _():
-            q1_copy(e).start()
-
-        return carry
-
-    lax.fori_loop(1, NY + 1, add1, 0)
-    for xt in range(NX):
-        for e in (1, 2, 3):
-            p2_copy(e, xt).wait_recv()
-
-    def add2(d, carry):
-        xt = (x + d) % NX
-        total = s2[y, xt].astype(F32) + r2[0, xt].astype(F32) + r2[1, xt].astype(F32) + r2[2, xt].astype(F32)
-        t2[xt] = total.astype(BF)
-
-        @pl.when(d != NX)
-        def _():
-            q2_copy(d).start()
-
-        return carry
-
-    lax.fori_loop(1, NX + 1, add2, 0)
+
+    def far_tile(i, carry):
+        grad_tile((x + i) % NX, 1 - yh)
+        return carry
+
+    lax.fori_loop(0, NX, far_tile, 0)
 
     for e in (1, 2, 3):
         q1_copy(e).wait_recv()
@@ -283,6 +303,8 @@
     total = t2[x].astype(F32) + u2[0].astype(F32) + u2[1].astype(F32) + u2[2].astype(F32)
     vb[:, :, 256:512] = total.astype(BF).reshape(8, 16, 256)
 
+    pl.semaphore_wait(four_sem, 2)
+
     def z_copy(k):
         return send(vb.at[k], zr.at[z // 2], z_s.at[k], z_r.at[z // 2], me(z=p * 8 + k))
 
@@ -303,7 +325,11 @@
 
     for j in (1, 2, 3):
         for xt in range(NX):
-            send(ngs.at[xt, :, pl.ds(0, T)], ngr.at[j, xt], back_s.at[0, xt], back_r.at[j - 1, xt], me(c=1 - c)).wait_recv()
+            for ht in range(2):
+                send(
+                    ngs.at[xt, ht, pl.ds(0, T)], ngr.at[j, xt, ht],
+                    back_s.at[0, xt, ht], back_r.at[j - 1, xt, ht], me(c=1 - c),
+                ).wait_recv()
 
     def feature_tile(j, xt, ht):
         return ngr[j, xt, ht].astype(F32) * gain_ref[:, pl.ds(column(j, xt, ht), F)]
@@ -324,12 +350,10 @@
         scale = jnp.concatenate([scale, scale], axis=1)
         for j in range(4):
             grad = scale * (feature_tile(j, xt, ht) - unit_tile(j, xt, ht) * spread)
-            outb[:, pl.ds(column(j, xt, ht), F)] = grad.astype(BF)
+            ig_ref[:, pl.ds(column(j, xt, ht), F)] = grad.astype(BF)
         return carry
 
     lax.fori_loop(0, 8, input_tile, 0)
-    store = pltpu.make_async_copy(outb, ig_hbm, out_sem.at[0])
-    store.start()
 
     def z_wait(k, carry):
         @pl.when(2 * k + z // 8 != z)
@@ -358,7 +382,8 @@
     for i in range(3):
         for xt in range(NX):
             token_copy(i, xt).wait_send()
-            back_copy(i, xt).wait_send()
+            for ht in range(2):
+                back_copy(i, xt, ht).wait_send()
             p2_copy(i + 1, xt).wait_send()
         for ht in range(2):
             p1_copy(i + 1, ht).wait_send()
@@ -373,24 +398,23 @@
         return carry
 
     lax.fori_loop(0, 8, z_sent, 0)
-    store.wait()
 
 
 def on_device(tokens_in, gain, value_weight, value_grad):
     vmem, dma = pltpu.VMEM, pltpu.SemaphoreType.DMA
     scratch = [
-        vmem((T, D), BF), vmem((K, K), BF), vmem((4 * T, K), BF), vmem((T, 128), F32),
+        vmem((T, D), BF), vmem((1, D), F32), vmem((K, K), BF), vmem((4 * T, K), BF), vmem((T, 128), F32),
         vmem((3, NX, 2, T, F), BF), vmem((NX, 2, 4 * T, F), BF), vmem((NX, 2, F, K), BF),
         vmem((NX, 2, 3 * T, F), BF), vmem((4, NX, 2, T, F), BF),
         vmem((NX, NY, 128, 256), BF), vmem((NY, NX, 128, 256), BF),
         vmem((3, NY, 128, 256), BF), vmem((3, NX, 128, 256), BF),
         vmem((NY, 128, 256), BF), vmem((NX, 128, 256), BF),
         vmem((3, 128, 256), BF), vmem((3, 128, 256), BF),
-        vmem((8, 16, K), BF), vmem((8, 16, K), BF), vmem((T, D), BF),
+        vmem((8, 16, K), BF), vmem((8, 16, K), BF),
     ]
-    sems = [(3,)] + [(3,)] * 2 + [(3, NX)] * 2 + [(3,)] * 2 + [(4,)] * 4 + [(3, NX)] * 2
-    sems += [(3, 2)] * 2 + [(3, NX)] * 2 + [(3,)] * 4 + [(8,)] * 2 + [(1,)]
-    any_space = pl.BlockSpec(memory_space=pl.ANY)
+    sems = [(4,)] + [(3,)] * 2 + [(3, NX)] * 2 + [(3,)] * 2 + [(4,)] * 4 + [(3, NX, 2)] * 2
+    sems += [(3, 2)] * 2 + [(3, NX)] * 2 + [(3,)] * 4 + [(8,)] * 2
+    in_hbm = pl.BlockSpec(memory_space=pltpu.HBM)
     in_vmem = pl.BlockSpec(memory_space=pltpu.VMEM)
     weight_grad, gain_grad, input_grad = pl.pallas_call(
         kernel,
@@ -399,13 +423,13 @@
             jax.ShapeDtypeStruct((1, 128), F32),
             jax.ShapeDtypeStruct((T, D), BF),
         ),
-        in_specs=[any_space, in_vmem, any_space, any_space],
-        out_specs=(in_vmem, in_vmem, any_space),
-        scratch_shapes=scratch + [dma(s) for s in sems],
+        in_specs=[in_hbm] * 4,
+        out_specs=(in_vmem, in_vmem, in_vmem),
+        scratch_shapes=scratch + [dma(s) for s in sems] + [pltpu.SemaphoreType.REGULAR] * 3,
         compiler_params=pltpu.CompilerParams(
-            collective_id=0, has_side_effects=True, vmem_limit_bytes=48 * 1024 * 1024
+            collective_id=0, has_side_effects=True, vmem_limit_bytes=40 * 1024 * 1024
         ),
-    )(tokens_in, gain.reshape(1, D), value_weight, value_grad)
+    )(*(pltpu.with_memory_space_constraint(a, pltpu.HBM) for a in (tokens_in, gain.reshape(1, D), value_weight, value_grad)))
     return weight_grad, gain_grad[0, :16], input_grad
 
 

time: 72 us -> 65.3 us (0.907)
  the two profiles are of different devices: /device:TPU:7 before, /device:TPU:10 now
where the time goes in v2:
time: 65.3 us; the launch traced here: 65.2 us
  Pallas kernels  62.1 us (95%)
  local copies, waits for them, and re-layouts  2.45 us (4%)
    pallas_call x1, Pallas kernels, on_device(): pl.pallas_call(kernel, out_shape=(jax.ShapeDtypeStruct((16, K), F32), jax...  62.1 us
    unnamed x2, local copies, waits for them, and re-layouts  1.93 us

profile of v2, /device:TPU:10, one launch (start us, length us, event | category | flops | bytes accessed | tf_op | source)
XLA Modules:
  0.0 65.2 jit_solution(18027585864253552780)
XLA Ops:
  0.6 62.1 %shard_map.67 = (f32[16,512]{1,0:T(8,128)S(1)}, f32[1,128]{1,0:T(1,128)S(1)}, bf16[128,8192]{1,0:T(8,128)(2,1)S(1)}) custom-call(bf16[128,8192]{1,0:T(8,128)(2,1)} %tok_hbm.1, f32[1,8192]{1,0:T(1,128)} %bitcast.3, bf16[512,512]{1,0:T(8,128)(2,1)} %weight_hbm.1, bf16[128,512]{1,0:T(8,128)(2,1)} %vg_hbm.1), custom_call_target="tpu_custom_call" | custom-call | tf_op jit(solution)/shard_map/pallas_call | solution.py:419
  62.8 0.5 slice_bitcast_fusion
  63.3 0.6 copy.9
  63.9 1.3 %copy.10 = bf16[128,8192]{1,0:T(8,128)(2,1)} copy(bf16[128,8192]{1,0:T(8,128)(2,1)S(1)} %get-tuple-element.14) | data formatting | bytes 4194304

commit v3 on v2

v3 whole, which is shorter than its diff:
```python
import jax
import jax.numpy as jnp
from jax import lax
from jax.experimental import pallas as pl
from jax.experimental.pallas import tpu as pltpu
from jax.sharding import PartitionSpec as P

D = 8192
EPS = 1e-05
NX, NY, NZ = 4, 4, 16
T = 128
K = 512
F = 256
BF, F32 = jnp.bfloat16, jnp.float32
MESH = pl.DeviceIdType.MESH
STEPS = (2, 0, 3, 1)


def device_at(x, y, z, core):
    return (x * 4 + (y // 2) * 2 + core, z * 2 + y % 2)


def kernel(
    tok_hbm, gain_hbm, weight_hbm, vg_hbm,
    wg_ref, gg_ref, ig_ref,
    tok, gain_ref, shard, vgraw, vgall, nall, wall, ngs, ngr,
    s1, s2, a1, a2, r1, r2, t1, t2, u1, u2, vb, zr,
    load_sem, vg_s, vg_r, tok_s, tok_r, ax_s, ax_r, ay_s, ay_r, ap_s, ap_r,
    back_s, back_r, a1_s, a1_r, a2_s, a2_r, p1_s, p1_r, p2_s, p2_r, q1_s, q1_r, q2_s, q2_r, z_s, z_r, near_sem, two_sem, four_sem,
):
    node, dp = lax.axis_index("node"), lax.axis_index("dp")
    x, yh, c = node // 4, (node // 2) % 2, node % 2
    z, yl = dp // 2, dp % 2
    y = yh * 2 + yl
    p = z % 2
    zs = (z + 17 - 2 * c) % NZ
    zup, zdn = (z + 1) % NZ, (z + 15) % NZ
    me = lambda **kw: device_at(kw.get("x", x), kw.get("y", y), kw.get("z", z), kw.get("c", c))

    def send(src, dst, ssem, rsem, to):
        return pltpu.make_async_remote_copy(
            src_ref=src, dst_ref=dst, send_sem=ssem, recv_sem=rsem, device_id=to, device_id_type=MESH
        )

    load_tok = pltpu.make_async_copy(tok_hbm, tok, load_sem.at[0])
    load_w = pltpu.make_async_copy(weight_hbm, shard, load_sem.at[1])
    load_vg = pltpu.make_async_copy(vg_hbm, vgraw, load_sem.at[2])
    load_gain = pltpu.make_async_copy(gain_hbm, gain_ref, load_sem.at[3])
    load_w.start()
    load_tok.start()
    load_vg.start()
    load_gain.start()

    barrier = pltpu.get_barrier_semaphore()
    partners = [me(x=(x + d) % NX) for d in (1, 2, 3)] + [me(y=(y + d) % NY) for d in (1, 2, 3)]
    partners += [me(c=1 - c), me(z=zup), me(z=zdn), me(z=zup, c=1 - c), me(z=zdn, c=1 - c)]
    for to in partners:
        pl.semaphore_signal(barrier, inc=1, device_id=to, device_id_type=MESH)

    def tell(sem, d):
        for to in (me(z=(z + d) % NZ), me(z=(z + NZ - d) % NZ)):
            pl.semaphore_signal(sem, inc=1, device_id=to, device_id_type=MESH)

    def column(j, xt, ht):
        cc = c if j in (0, 2) else 1 - c
        pp = p if j < 2 else 1 - p
        return pl.multiple_of(xt * 2048 + ht * 1024 + cc * 512 + pp * 256, 256)

    load_w.wait()
    pl.semaphore_wait(barrier, len(partners))
    tell(near_sem, 1)

    own_rows = pl.ds(pl.multiple_of(p * F, F), F)
    half = 1 - yl
    out_half = pl.ds(pl.multiple_of(half * 128, 128), 128)
    in_half = pl.ds(pl.multiple_of(yl * 128, 128), 128)
    def shard_half(h):
        return shard.at[pl.ds(pl.multiple_of(p * F + h * 128, 128), 128)]

    axo, axi = [
        [
            send(shard_half(h), wall.at[x, yh, rows], ax_s.at[k, d - 1], ax_r.at[k, d - 1], me(x=(x + d) % NX))
            for d in (1, 2, 3)
        ]
        for k, (h, rows) in enumerate(((half, out_half), (yl, in_half)))
    ]
    ay = [
        send(
            shard.at[own_rows] if d == 0 else wall.at[(x + d) % NX, yh, out_half],
            wall.at[x, yh] if d == 0 else wall.at[(x + d) % NX, yh, out_half], ay_s.at[d], ay_r.at[d], me(y=3 - y),
        )
        for d in range(NX)
    ]
    ap = {
        d: send(
            wall.at[(x + d) % NX, 1 - yh, in_half], wall.at[(x + d) % NX, 1 - yh, in_half],
            ap_s.at[d], ap_r.at[d], me(y=yh * 2 + 1 - yl),
        )
        for d in (1, 2, 3)
    }
    ay_in = [
        send(
            wall.at[x, 1 - yh] if d == 0 else wall.at[(x + d) % NX, 1 - yh, in_half],
            wall.at[x, 1 - yh] if d == 0 else wall.at[(x + d) % NX, 1 - yh, in_half],
            ay_s.at[d], ay_r.at[d], me(y=3 - y),
        )
        for d in range(NX)
    ]

    slot = 3 - c
    helpers = [(me(c=1 - c), 1), (me(z=zs), slot), (me(z=zs, c=1 - c), slot)]

    def token_copy(i, xt, ht):
        to, sl = helpers[i]
        return send(
            tok_hbm.at[:, pl.ds(column(i + 1, xt, ht), F)], nall.at[xt, ht, pl.ds(sl * T, T)],
            tok_s.at[i, xt, ht], tok_r.at[sl - 1, xt, ht], to,
        )

    def token_sends(m, carry):
        xt = (x + STEPS[m]) % NX
        for ht in range(2):
            for i in range(3):
                token_copy(i, xt, ht).start()
        return carry

    token_sends(0, 0)
    ay[0].start()
    for i in (0, 2, 1):
        axo[i].start()
    load_tok.wait()

    def squares(i, acc):
        t = tok[:, pl.ds(pl.multiple_of(i * K, K), K)].astype(F32)
        t = t * t
        return acc + ((t[:, 0:128] + t[:, 128:256]) + (t[:, 256:384] + t[:, 384:512]))

    acc = lax.fori_loop(0, D // K, squares, jnp.zeros((T, 128), F32))
    mean_square = jnp.sum(acc, axis=1, keepdims=True) * (1.0 / D)
    inv_rms = lax.rsqrt(mean_square + EPS)
    load_vg.wait()
    vgall[0:T] = (vgraw[...].astype(F32) * inv_rms).astype(BF)

    def vg_copy(i, mine, to_slot, to):
        return send(
            vgall.at[pl.ds(mine * T, T)], vgall.at[pl.ds(to_slot * T, T)], vg_s.at[i], vg_r.at[to_slot - 1], to
        )

    vg_copies = [vg_copy(0, 0, 1, me(c=1 - c)), vg_copy(1, 0, slot, me(z=zs)), vg_copy(2, slot, slot, me(c=1 - c))]
    vg_copies[0].start()
    vg_copies[1].start()
    token_sends(1, 0)
    wall[x, yh] = shard[own_rows]

    def own_tokens(i, carry):
        nall[i // 2, i % 2, 0:T] = tok[:, pl.ds(column(0, i // 2, i % 2), F)]
        return carry

    lax.fori_loop(0, 8, own_tokens, 0)
    load_gain.wait()

    axo[0].wait_recv()
    ay[3].start()
    axo[2].wait_recv()
    ay[1].start()
    token_sends(2, 0)
    axi[0].start()
    axi[2].start()

    vg_copy(1, 0, slot, me(z=zs)).wait_recv()
    vg_copies[2].start()
    pl.semaphore_wait(near_sem, 2)
    tell(two_sem, 2)
    for sl in (1, 2 + c):
        vg_copy(0, 0, sl, me(c=1 - c)).wait_recv()

    def a1_copy(ht):
        return send(
            s1.at[(x + 2) % NX, pl.ds(ht * 2, 2)], a1.at[ht], a1_s.at[ht], a1_r.at[ht], me(x=(x + (1, 3)[ht]) % NX)
        )

    def a2_copy(m):
        xt = (x + STEPS[m]) % NX
        return send(s2.at[(y + 2) % NY, xt], a2.at[m], a2_s.at[m], a2_r.at[m], me(y=(y + (1, 3)[m % 2]) % NY))

    def p1_copy(d, ht):
        return send(
            s1.at[(x + d) % NX, pl.ds(ht * 2, 2)], r1.at[d // 2, pl.ds(ht * 2, 2)],
            p1_s.at[d // 2, ht], p1_r.at[d // 2, ht], me(x=(x + d) % NX),
        )

    def p2_copy(e, m):
        xt = (x + STEPS[m]) % NX
        return send(
            s2.at[(y + e) % NY, xt], r2.at[e // 2, xt], p2_s.at[e // 2, m], p2_r.at[e // 2, m], me(y=(y + e) % NY)
        )

    def weight_tile(xt, ht):
        total = lax.dot_general(nall[xt, ht], vgall[...], (((0,), (0,)), ((), ())), preferred_element_type=F32)
        total = total.astype(BF).reshape(8, 2, 16, K)
        for low in range(2):
            part = total[:, low].reshape(128, K)
            s1[xt, ht * 2 + low] = part[:, 0:256]
            s2[ht * 2 + low, xt] = part[:, 256:512]

    def weight_step(m):
        d = STEPS[m]
        xt = (x + d) % NX
        for ht in range(2):
            for sl in (1, 2, 3):
                send(
                    nall.at[xt, ht, pl.ds(0, T)], nall.at[xt, ht, pl.ds(sl * T, T)],
                    tok_s.at[0, xt, ht], tok_r.at[sl - 1, xt, ht], me(c=1 - c),
                ).wait_recv()
            weight_tile(xt, ht)
            if d == 2:
                a1_copy(ht).start()
            elif d != 0:
                if (d, ht) in ((1, 0), (3, 1)):
                    a1_copy(ht).wait_recv()
                    rows = pl.ds(ht * 2, 2)
                    s1[xt, rows] = (s1[xt, rows].astype(F32) + a1[ht].astype(F32)).astype(BF)
                p1_copy(d, ht).start()
        a2_copy(m).start()
        p2_copy((3, 1)[m % 2], m).start()

    def relay(m):
        e, xt = (1, 3)[m % 2], (x + STEPS[m]) % NX
        yt = (y + e) % NY
        a2_copy(m).wait_recv()
        s2[yt, xt] = (s2[yt, xt].astype(F32) + a2[m].astype(F32)).astype(BF)
        p2_copy(e, m).start()

    owners = [(me(c=1 - c), 1), (me(z=zup, c=1), 3 - c), (me(z=zdn, c=0), 2 + c)]

    def back_copy(i, xt, ht):
        to, j = owners[i]
        return send(
            ngs.at[xt, ht, pl.ds(i * T, T)], ngr.at[j, xt, ht], back_s.at[i, xt, ht], back_r.at[j - 1, xt, ht], to
        )

    def grad_tile(xt, ht):
        ng = lax.dot_general(
            vgall[...], wall[xt, ht], (((1,), (1,)), ((), ())), preferred_element_type=F32
        ).astype(BF)
        ngr[0, xt, ht] = ng[0:T]
        ngs[xt, ht] = ng[T:]
        for i in range(3):
            back_copy(i, xt, ht).start()

    weight_step(0)
    token_sends(3, 0)
    pl.semaphore_wait(two_sem, 2)
    tell(four_sem, 4)
    axo[1].wait_recv()
    ay[2].start()
    axi[1].start()
    weight_step(1)
    ay_in[3].wait_recv()
    ap[3].start()
    weight_step(2)
    relay(0)
    ay_in[1].wait_recv()
    ap[1].start()
    weight_step(3)
    relay(1)
    ay_in[2].wait_recv()
    ap[2].start()
    for copy in axi:
        copy.wait_recv()

    def near_tile(i, carry):
        grad_tile((x + i) % NX, yh)
        return carry

    lax.fori_loop(0, NX, near_tile, 0)
    ay_in[0].wait_recv()
    grad_tile(x, 1 - yh)

    def q1_copy(e):
        return send(t1.at[(y + e) % NY], u1.at[e - 1], q1_s.at[e - 1], q1_r.at[e - 1], me(y=(y + e) % NY))

    def q2_copy(d):
        return send(t2.at[(x + d) % NX], u2.at[d - 1], q2_s.at[d - 1], q2_r.at[d - 1], me(x=(x + d) % NX))

    for m in (2, 3):
        relay(m)
    for ht in range(2):
        for d in (1, 3):
            p1_copy(d, ht).wait_recv()

    def add1(e, carry):
        yt = (y + e) % NY
        total = s1[x, yt].astype(F32) + r1[0, yt].astype(F32) + r1[1, yt].astype(F32)
        t1[yt] = total.astype(BF)

        @pl.when(e != NY)
        def _():
            q1_copy(e).start()

        return carry

    lax.fori_loop(1, NY + 1, add1, 0)
    for m in range(NX):
        for e in (1, 3):
            p2_copy(e, m).wait_recv()

    def add2(d, carry):
        xt = (x + d) % NX
        total = s2[y, xt].astype(F32) + r2[0, xt].astype(F32) + r2[1, xt].astype(F32)
        t2[xt] = total.astype(BF)

        @pl.when(d != NX)
        def _():
            q2_copy(d).start()

        return carry

    lax.fori_loop(1, NX + 1, add2, 0)

    for d in (3, 1, 2):
        send(
            wall.at[(x + d) % NX, 1 - yh, out_half], wall.at[(x + d) % NX, 1 - yh, out_half],
            ap_s.at[d], ap_r.at[d], me(y=yh * 2 + 1 - yl),
        ).wait_recv()
        grad_tile((x + d) % NX, 1 - yh)

    for e in (1, 2, 3):
        q1_copy(e).wait_recv()
    total = t1[y].astype(F32) + u1[0].astype(F32) + u1[1].astype(F32) + u1[2].astype(F32)
    vb[:, :, 0:256] = total.astype(BF).reshape(8, 16, 256)
    for d in (1, 2, 3):
        q2_copy(d).wait_recv()
    total = t2[x].astype(F32) + u2[0].astype(F32) + u2[1].astype(F32) + u2[2].astype(F32)
    vb[:, :, 256:512] = total.astype(BF).reshape(8, 16, 256)

    pl.semaphore_wait(four_sem, 2)

    def z_copy(k):
        return send(vb.at[k], zr.at[z // 2], z_s.at[k], z_r.at[z // 2], me(z=p * 8 + k))

    def z_start(i, carry):
        k = (z + i) % 8

        @pl.when(p * 8 + k != z)
        def _():
            z_copy(k).start()

        @pl.when(p * 8 + k == z)
        def _():
            zr[z // 2] = vb[k]

        return carry

    lax.fori_loop(0, 8, z_start, 0)

    for j in (1, 2, 3):
        for xt in range(NX):
            for ht in range(2):
                send(
                    ngs.at[xt, ht, pl.ds(0, T)], ngr.at[j, xt, ht],
                    back_s.at[0, xt, ht], back_r.at[j - 1, xt, ht], me(c=1 - c),
                ).wait_recv()

    def feature_tile(j, xt, ht):
        return ngr[j, xt, ht].astype(F32) * gain_ref[:, pl.ds(column(j, xt, ht), F)]

    def token_tile(j, xt, ht):
        return tok[:, pl.ds(column(j, xt, ht), F)].astype(F32)

    def spread_tile(i, acc):
        xt, ht = i // 2, i % 2
        for j in range(4):
            prod = feature_tile(j, xt, ht) * token_tile(j, xt, ht)
            acc = acc + (prod[:, 0:128] + prod[:, 128:256])
        return acc

    acc = lax.fori_loop(0, 8, spread_tile, jnp.zeros((T, 128), F32))
    spread = jnp.sum(acc, axis=1, keepdims=True) * (1.0 / D) * (inv_rms * inv_rms)

    def input_tile(i, carry):
        xt, ht = i // 2, i % 2
        for j in range(4):
            grad = feature_tile(j, xt, ht) - token_tile(j, xt, ht) * spread
            ig_ref[:, pl.ds(column(j, xt, ht), F)] = grad.astype(BF)
        return carry

    lax.fori_loop(0, 8, input_tile, 0)

    def z_wait(k, carry):
        @pl.when(2 * k + z // 8 != z)
        def _():
            send(vb.at[k], zr.at[k], z_s.at[k], z_r.at[k], me(z=(z + 1) % NZ)).wait_recv()

        return carry

    lax.fori_loop(0, 8, z_wait, 0)
    total = zr[0].astype(F32)
    for k in range(1, 8):
        total = total + zr[k].astype(F32)

    lanes = lax.broadcasted_iota(jnp.int32, (16, 128), 1)
    rows = lax.broadcasted_iota(jnp.int32, (16, 128), 0)
    block = gain_ref[:, pl.ds(pl.multiple_of(node * 512 + (dp // 8) * 128, 128), 128)]
    picked = jnp.where(lanes == rows + (dp % 8) * 16, jnp.broadcast_to(block, (16, 128)), 0.0)
    wg_ref[...] = total * jnp.sum(picked, axis=1, keepdims=True)
    own = shard[pl.ds(pl.multiple_of(dp * 16, 16), 16)].astype(F32)
    gain_sum = jnp.sum(own * total, axis=1, keepdims=True)
    spread_out = jnp.where(lanes == rows, jnp.broadcast_to(gain_sum, (16, 128)), 0.0)
    gg_ref[...] = jnp.sum(spread_out, axis=0, keepdims=True)

    for copy in vg_copies + axo + axi + ay + [ap[1], ap[2], ap[3]]:
        copy.wait_send()
    for i in range(3):
        for xt in range(NX):
            for ht in range(2):
                token_copy(i, xt, ht).wait_send()
                back_copy(i, xt, ht).wait_send()
        q1_copy(i + 1).wait_send()
        q2_copy(i + 1).wait_send()

    for ht in range(2):
        a1_copy(ht).wait_send()
        for d in (1, 3):
            p1_copy(d, ht).wait_send()
    for m in range(NX):
        a2_copy(m).wait_send()
        for e in (1, 3):
            p2_copy(e, m).wait_send()

    def z_sent(k, carry):
        @pl.when(p * 8 + k != z)
        def _():
            z_copy(k).wait_send()

        return carry

    lax.fori_loop(0, 8, z_sent, 0)


def on_device(tokens_in, gain, value_weight, value_grad):
    vmem, dma = pltpu.VMEM, pltpu.SemaphoreType.DMA
    scratch = [
        vmem((T, D), BF), vmem((1, D), F32), vmem((K, K), BF), vmem((T, K), BF), vmem((4 * T, K), BF),
        vmem((NX, 2, 4 * T, F), BF), vmem((NX, 2, F, K), BF),
        vmem((NX, 2, 3 * T, F), BF), vmem((4, NX, 2, T, F), BF),
        vmem((NX, NY, 128, 256), BF), vmem((NY, NX, 128, 256), BF),
        vmem((2, 2, 128, 256), BF), vmem((NX, 128, 256), BF),
        vmem((2, NY, 128, 256), BF), vmem((2, NX, 128, 256), BF),
        vmem((NY, 128, 256), BF), vmem((NX, 128, 256), BF),
        vmem((3, 128, 256), BF), vmem((3, 128, 256), BF),
        vmem((8, 16, K), BF), vmem((8, 16, K), BF),
    ]
    sems = [(4,)] + [(3,)] * 2 + [(3, NX, 2)] * 2 + [(2, 3)] * 2 + [(4,)] * 4 + [(3, NX, 2)] * 2
    sems += [(2,)] * 2 + [(NX,)] * 2 + [(2, 2)] * 2 + [(2, NX)] * 2 + [(3,)] * 4 + [(8,)] * 2
    operands = (tokens_in, gain.reshape(1, D), value_weight, value_grad)
    operands = [pltpu.with_memory_space_constraint(a, pltpu.HBM) for a in operands]
    in_hbm = pl.BlockSpec(memory_space=pltpu.HBM)
    in_vmem = pl.BlockSpec(memory_space=pltpu.VMEM)
    weight_grad, gain_grad, input_grad = pl.pallas_call(
        kernel,
        out_shape=(
            jax.ShapeDtypeStruct((16, K), F32),
            jax.ShapeDtypeStruct((1, 128), F32),
            jax.ShapeDtypeStruct((T, D), BF),
        ),
        in_specs=[in_hbm] * 4,
        out_specs=(in_vmem, in_vmem, in_vmem),
        scratch_shapes=scratch + [dma(s) for s in sems] + [pltpu.SemaphoreType.REGULAR] * 3,
        compiler_params=pltpu.CompilerParams(
            collective_id=0, has_side_effects=True, vmem_limit_bytes=40 * 1024 * 1024
        ),
    )(*operands)
    return weight_grad, gain_grad[0, :16], input_grad


def solution(mesh):
    placed = (P(("node", "dp"), None), P(), P("node", None), P(("node", "dp"), None))
    return jax.shard_map(
        on_device,
        mesh=mesh,
        in_specs=placed,
        out_specs=(P(("node", "dp"), None), P(("node", "dp")), P(("node", "dp"), None)),
        check_vma=False,
    )
```

time: 65.3 us -> 59.9 us (0.917)
  the two profiles are of different devices: /device:TPU:10 before, /device:TPU:32 now
where the time goes in v3:
time: 59.9 us; the launch traced here: 59.8 us
  Pallas kernels  56.7 us (95%)
  local copies, waits for them, and re-layouts  2.45 us (4%)
  between operations  0.64 us (1%)
    pallas_call x1, Pallas kernels, on_device(): pl.pallas_call(kernel, out_shape=(jax.ShapeDtypeStruct((16, K), F32), jax...  56.7 us
    unnamed x2, local copies, waits for them, and re-layouts  1.93 us

profile of v3, /device:TPU:32, one launch (start us, length us, event | category | flops | bytes accessed | tf_op | source)
XLA Modules:
  0.0 59.8 jit_solution(6225345308995120811)
XLA Ops:
  0.6 56.7 %shard_map.67 = (f32[16,512]{1,0:T(8,128)S(1)}, f32[1,128]{1,0:T(1,128)S(1)}, bf16[128,8192]{1,0:T(8,128)(2,1)S(1)}) custom-call(bf16[128,8192]{1,0:T(8,128)(2,1)} %tok_hbm.1, f32[1,8192]{1,0:T(1,128)} %bitcast.3, bf16[512,512]{1,0:T(8,128)(2,1)} %weight_hbm.1, bf16[128,512]{1,0:T(8,128)(2,1)} %vg_hbm.1), custom_call_target="tpu_custom_call" | custom-call | tf_op jit(solution)/shard_map/pallas_call | solution.py:460
  57.3 0.5 slice_bitcast_fusion
  57.8 0.6 %copy.9 = f32[16,512]{1,0:T(8,128)} copy(f32[16,512]{1,0:T(8,128)S(1)} %get-tuple-element.12) | data formatting | bytes 65536
  58.4 1.3 %copy.10 = bf16[128,8192]{1,0:T(8,128)(2,1)} copy(bf16[128,8192]{1,0:T(8,128)(2,1)S(1)} %get-tuple-element.14) | data formatting | bytes 4194304

commit v4 on v3

--- a/solution.py
+++ b/solution.py
@@ -23,9 +23,9 @@
 def kernel(
     tok_hbm, gain_hbm, weight_hbm, vg_hbm,
     wg_ref, gg_ref, ig_ref,
-    tok, gain_ref, shard, vgraw, vgall, nall, wall, ngs, ngr,
+    tok, gain_ref, shard, vgraw, vgall, invs, nall, wall, ngs, ngr,
     s1, s2, a1, a2, r1, r2, t1, t2, u1, u2, vb, zr,
-    load_sem, vg_s, vg_r, tok_s, tok_r, ax_s, ax_r, ay_s, ay_r, ap_s, ap_r,
+    load_sem, vg_s, vg_r, inv_s, inv_r, tok_s, tok_r, ax_s, ax_r, ay_s, ay_r, ap_s, ap_r,
     back_s, back_r, a1_s, a1_r, a2_s, a2_r, p1_s, p1_r, p2_s, p2_r, q1_s, q1_r, q2_s, q2_r, z_s, z_r, near_sem, two_sem, four_sem,
 ):
     node, dp = lax.axis_index("node"), lax.axis_index("dp")
@@ -44,11 +44,11 @@
 
     load_tok = pltpu.make_async_copy(tok_hbm, tok, load_sem.at[0])
     load_w = pltpu.make_async_copy(weight_hbm, shard, load_sem.at[1])
-    load_vg = pltpu.make_async_copy(vg_hbm, vgraw, load_sem.at[2])
+    load_vg = pltpu.make_async_copy(vg_hbm, vgraw.at[pl.ds(0, T)], load_sem.at[2])
     load_gain = pltpu.make_async_copy(gain_hbm, gain_ref, load_sem.at[3])
+    load_vg.start()
     load_w.start()
     load_tok.start()
-    load_vg.start()
     load_gain.start()
 
     barrier = pltpu.get_barrier_semaphore()
@@ -117,14 +117,26 @@
             tok_s.at[i, xt, ht], tok_r.at[sl - 1, xt, ht], to,
         )
 
-    def token_sends(m, carry):
+    def token_sends(m, tiles=(0, 1)):
         xt = (x + STEPS[m]) % NX
-        for ht in range(2):
+        for ht in tiles:
             for i in range(3):
                 token_copy(i, xt, ht).start()
-        return carry
-
-    token_sends(0, 0)
+
+    def vg_copy(i, mine, to_slot, to):
+        return send(
+            vgraw.at[pl.ds(mine * T, T)], vgraw.at[pl.ds(to_slot * T, T)], vg_s.at[i], vg_r.at[to_slot - 1], to
+        )
+
+    def inv_copy(i):
+        to, sl = helpers[i]
+        return send(invs.at[0], invs.at[sl], inv_s.at[i], inv_r.at[sl - 1], to)
+
+    vg_copies = [vg_copy(0, 0, 1, me(c=1 - c)), vg_copy(1, 0, slot, me(z=zs)), vg_copy(2, slot, slot, me(c=1 - c))]
+    load_vg.wait()
+    vg_copies[0].start()
+    vg_copies[1].start()
+    token_sends(0, (0,))
     ay[0].start()
     for i in (0, 2, 1):
         axo[i].start()
@@ -138,18 +150,11 @@
     acc = lax.fori_loop(0, D // K, squares, jnp.zeros((T, 128), F32))
     mean_square = jnp.sum(acc, axis=1, keepdims=True) * (1.0 / D)
     inv_rms = lax.rsqrt(mean_square + EPS)
-    load_vg.wait()
-    vgall[0:T] = (vgraw[...].astype(F32) * inv_rms).astype(BF)
-
-    def vg_copy(i, mine, to_slot, to):
-        return send(
-            vgall.at[pl.ds(mine * T, T)], vgall.at[pl.ds(to_slot * T, T)], vg_s.at[i], vg_r.at[to_slot - 1], to
-        )
-
-    vg_copies = [vg_copy(0, 0, 1, me(c=1 - c)), vg_copy(1, 0, slot, me(z=zs)), vg_copy(2, slot, slot, me(c=1 - c))]
-    vg_copies[0].start()
-    vg_copies[1].start()
-    token_sends(1, 0)
+    invs[0] = jnp.broadcast_to(inv_rms, (T, 128)).T[0:8]
+    for i in range(3):
+        inv_copy(i).start()
+    token_sends(0, (1,))
+    token_sends(1)
     wall[x, yh] = shard[own_rows]
 
     def own_tokens(i, carry):
@@ -159,20 +164,26 @@
     lax.fori_loop(0, 8, own_tokens, 0)
     load_gain.wait()
 
+    vg_copy(1, 0, slot, me(z=zs)).wait_recv()
+    vg_copies[2].start()
     axo[0].wait_recv()
     ay[3].start()
     axo[2].wait_recv()
     ay[1].start()
-    token_sends(2, 0)
+    token_sends(2)
     axi[0].start()
     axi[2].start()
 
-    vg_copy(1, 0, slot, me(z=zs)).wait_recv()
-    vg_copies[2].start()
     pl.semaphore_wait(near_sem, 2)
     tell(two_sem, 2)
     for sl in (1, 2 + c):
         vg_copy(0, 0, sl, me(c=1 - c)).wait_recv()
+    for sl in (1, 2, 3):
+        send(invs.at[0], invs.at[sl], inv_s.at[0], inv_r.at[sl - 1], me(c=1 - c)).wait_recv()
+    for sl in range(4):
+        scale = jnp.concatenate([invs[sl]] * 16, axis=0).T[:, 0:1]
+        rows = pl.ds(sl * T, T)
+        vgall[rows] = (vgraw[rows].astype(F32) * scale).astype(BF)
 
     def a1_copy(ht):
         return send(
@@ -249,7 +260,7 @@
             back_copy(i, xt, ht).start()
 
     weight_step(0)
-    token_sends(3, 0)
+    token_sends(3)
     pl.semaphore_wait(two_sem, 2)
     tell(four_sem, 4)
     axo[1].wait_recv()
@@ -354,9 +365,9 @@
 
     lax.fori_loop(0, 8, z_start, 0)
 
-    for j in (1, 2, 3):
-        for xt in range(NX):
-            for ht in range(2):
+    def returned(ht):
+        for j in (1, 2, 3):
+            for xt in range(NX):
                 send(
                     ngs.at[xt, ht, pl.ds(0, T)], ngr.at[j, xt, ht],
                     back_s.at[0, xt, ht], back_r.at[j - 1, xt, ht], me(c=1 - c),
@@ -368,14 +379,19 @@
     def token_tile(j, xt, ht):
         return tok[:, pl.ds(column(j, xt, ht), F)].astype(F32)
 
-    def spread_tile(i, acc):
-        xt, ht = i // 2, i % 2
-        for j in range(4):
-            prod = feature_tile(j, xt, ht) * token_tile(j, xt, ht)
-            acc = acc + (prod[:, 0:128] + prod[:, 128:256])
-        return acc
-
-    acc = lax.fori_loop(0, 8, spread_tile, jnp.zeros((T, 128), F32))
+    def add_spread(ht, acc):
+        def spread_tile(xt, acc):
+            for j in range(4):
+                prod = feature_tile(j, xt, ht) * token_tile(j, xt, ht)
+                acc = acc + (prod[:, 0:128] + prod[:, 128:256])
+            return acc
+
+        return lax.fori_loop(0, NX, spread_tile, acc)
+
+    returned(yh)
+    acc = add_spread(yh, jnp.zeros((T, 128), F32))
+    returned(1 - yh)
+    acc = add_spread(1 - yh, acc)
     spread = jnp.sum(acc, axis=1, keepdims=True) * (1.0 / D) * (inv_rms * inv_rms)
 
     def input_tile(i, carry):
@@ -412,6 +428,7 @@
     for copy in vg_copies + axo + axi + ay + [ap[1], ap[2], ap[3]]:
         copy.wait_send()
     for i in range(3):
+        inv_copy(i).wait_send()
         for xt in range(NX):
             for ht in range(2):
                 token_copy(i, xt, ht).wait_send()
@@ -441,7 +458,7 @@
 def on_device(tokens_in, gain, value_weight, value_grad):
     vmem, dma = pltpu.VMEM, pltpu.SemaphoreType.DMA
     scratch = [
-        vmem((T, D), BF), vmem((1, D), F32), vmem((K, K), BF), vmem((T, K), BF), vmem((4 * T, K), BF),
+        vmem((T, D), BF), vmem((1, D), F32), vmem((K, K), BF), vmem((4 * T, K), BF), vmem((4 * T, K), BF), vmem((4, 8, 128), F32),
         vmem((NX, 2, 4 * T, F), BF), vmem((NX, 2, F, K), BF),
         vmem((NX, 2, 3 * T, F), BF), vmem((4, NX, 2, T, F), BF),
         vmem((NX, NY, 128, 256), BF), vmem((NY, NX, 128, 256), BF),
@@ -451,7 +468,7 @@
         vmem((3, 128, 256), BF), vmem((3, 128, 256), BF),
         vmem((8, 16, K), BF), vmem((8, 16, K), BF),
     ]
-    sems = [(4,)] + [(3,)] * 2 + [(3, NX, 2)] * 2 + [(2, 3)] * 2 + [(4,)] * 4 + [(3, NX, 2)] * 2
+    sems = [(4,)] + [(3,)] * 4 + [(3, NX, 2)] * 2 + [(2, 3)] * 2 + [(4,)] * 4 + [(3, NX, 2)] * 2
     sems += [(2,)] * 2 + [(NX,)] * 2 + [(2, 2)] * 2 + [(2, NX)] * 2 + [(3,)] * 4 + [(8,)] * 2
     operands = (tokens_in, gain.reshape(1, D), value_weight, value_grad)
     operands = [pltpu.with_memory_space_constraint(a, pltpu.HBM) for a in operands]

time: 59.9 us -> 59.7 us (level)
  the two profiles are of different devices: /device:TPU:32 before, /device:TPU:20 now
where the time goes in v4:
time: 59.7 us; the launch traced here: 59.5 us
  Pallas kernels  56.4 us (94%)
  local copies, waits for them, and re-layouts  2.45 us (4%)
  between operations  0.64 us (1%)
    pallas_call x1, Pallas kernels, on_device(): pl.pallas_call(kernel, out_shape=(jax.ShapeDtypeStruct((16, K), F32), jax...  56.4 us
    unnamed x2, local copies, waits for them, and re-layouts  1.93 us

profile of v4, /device:TPU:20, one launch (start us, length us, event | category | flops | bytes accessed | tf_op | source)
XLA Modules:
  0.0 59.5 jit_solution(18253021147249973015)
XLA Ops:
  0.6 56.4 %shard_map.67 = (f32[16,512]{1,0:T(8,128)S(1)}, f32[1,128]{1,0:T(1,128)S(1)}, bf16[128,8192]{1,0:T(8,128)(2,1)S(1)}) custom-call(bf16[128,8192]{1,0:T(8,128)(2,1)} %tok_hbm.1, f32[1,8192]{1,0:T(1,128)} %bitcast.3, bf16[512,512]{1,0:T(8,128)(2,1)} %weight_hbm.1, bf16[128,512]{1,0:T(8,128)(2,1)} %vg_hbm.1), custom_call_target="tpu_custom_call" | custom-call | tf_op jit(solution)/shard_map/pallas_call | solution.py:477
  57.1 0.5 slice_bitcast_fusion
  57.6 0.6 %copy.9 = f32[16,512]{1,0:T(8,128)} copy(f32[16,512]{1,0:T(8,128)S(1)} %get-tuple-element.12) | data formatting | bytes 65536
  58.2 1.3 %copy.10 = bf16[128,8192]{1,0:T(8,128)(2,1)} copy(bf16[128,8192]{1,0:T(8,128)(2,1)S(1)} %get-tuple-element.14) | data formatting | bytes 4194304
